TPU v7x, 32 devices: a whole 2x2x4 slice. The times are simulated.
32 devices in a mesh: ctx: 8 (over z, x), head: 4 (over y, core).
Axes of the slice: x: 2, y: 2, z: 4, core: 2. Of those that a mesh axis runs over, the one named last changes fastest.
Arguments:
- projected: bfloat16 [3, 4096, 4096], P(None, ('ctx', 'head')), may hold values from -2.5 to 2.5
- conv_filter: float32 [3, 4, 4096], replicated, may hold values from -2.7 to 2.7
- frequencies: bfloat16 [32, 128, 256], replicated, may hold values from -5 to 5
Outputs:
- attended: bfloat16 [4096, 4096], P(('ctx', 'head'))
All inputs are finite; a program needn't handle non-finite values.
Results may differ from a plain program's by a relative error of at most 0.013.
Values may be sent and summed in bfloat16 or wider, within the bound.
A program may use at most 384 MiB of HBM per device.

v0:
```python
import jax
import jax.numpy as jnp
from jax import lax
from jax.sharding import PartitionSpec as P

H = 32
DH = 128
M = 256
KC = 4
BLOCK = 512


def passed_along(array, axis, by):
    size = lax.axis_size(axis)
    pairs = [(i, i + by) for i in range(size) if 0 <= i + by < size]
    return lax.ppermute(array, axis, pairs)


def prefix(array, axis, join, neutral):
    place = lax.axis_index(axis)
    gathered = jax.tree.map(
        lambda a, kind: lax.all_gather(a.astype(kind), axis), array, (jnp.bfloat16, jnp.bfloat16)
    )
    state = jax.tree.map(lambda a, e: jnp.zeros_like(a) + jnp.asarray(e, a.dtype), array, neutral)

    def one(step, state):
        return join(
            state,
            jax.tree.map(
                lambda a, own: lax.dynamic_index_in_dim(a, step, 0, False).astype(own.dtype),
                gathered,
                array,
            ),
        )

    return lax.fori_loop(0, place, one, state)


def convolve(padded, conv_taps, row_count):
    summed = jnp.zeros((padded.shape[0], row_count, padded.shape[2]), jnp.float32)
    for offset in range(KC):
        window = padded[:, KC - 1 - offset : KC - 1 - offset + row_count, :]
        summed = summed + conv_taps[:, offset][:, None, :] * window.astype(jnp.float32)
    return summed.astype(jnp.bfloat16)


def feature_maps(conved, head_omega, head_count):
    row_count = conved.shape[1]
    per_head = conved.reshape(3, row_count, head_count, DH)
    feature_scale = DH ** (-0.25)
    query_part = jnp.einsum(
        "lhd,hdm->lhm", per_head[0], head_omega, preferred_element_type=jnp.float32
    )
    query_map = jnp.exp(query_part * feature_scale).astype(jnp.bfloat16)
    keys_wide = per_head[1].astype(jnp.float32)
    halfnorm = jnp.sum(keys_wide * keys_wide, axis=2, keepdims=True) * (
        0.5 * feature_scale * feature_scale
    )
    key_part = jnp.einsum(
        "lhd,hdm->lhm", per_head[1], head_omega, preferred_element_type=jnp.float32
    )
    key_map = jnp.exp(key_part * feature_scale - halfnorm).astype(jnp.bfloat16)
    return (query_map, key_map, per_head[2])


def block_sums(key_map, values, block_rows):
    length, head_count = (key_map.shape[0], key_map.shape[1])
    block_count = length // block_rows
    key_blocks = key_map.reshape(block_count, block_rows, head_count, M)
    value_blocks = values.reshape(block_count, block_rows, head_count, DH)
    states = jnp.einsum(
        "brhm,brhd->bhmd", key_blocks, value_blocks, preferred_element_type=jnp.float32
    )
    totals = jnp.sum(key_blocks.astype(jnp.float32), axis=1)
    return (states, totals)


def split_pair(wide):
    upper = lax.optimization_barrier(wide.astype(jnp.bfloat16))
    lower = (wide - upper.astype(jnp.float32)).astype(jnp.bfloat16)
    return (upper, lower)


def attend(query_map, key_map, values, states, totals, prior_state, prior_total, block_rows):
    length, head_count = (query_map.shape[0], query_map.shape[1])
    block_count = length // block_rows
    causal = jnp.arange(block_rows)[:, None] >= jnp.arange(block_rows)[None, :]

    def advance(carried, pieces):
        running_state_sum, key_total = carried
        block_of_queries, block_of_keys, value_block, block_state, block_total = pieces
        scores = jnp.einsum(
            "qhm,khm->hqk", block_of_queries, block_of_keys, preferred_element_type=jnp.float32
        )
        scores = jnp.where(causal[None], scores, 0.0).astype(jnp.bfloat16)
        numerator = jnp.einsum(
            "hqk,khd->qhd", scores, value_block, preferred_element_type=jnp.float32
        )
        upper_state_part, lower_state_part = split_pair(running_state_sum)
        numerator = numerator + jnp.einsum(
            "tyg,ygl->tyl", block_of_queries, upper_state_part, preferred_element_type=jnp.float32
        )
        numerator = numerator + jnp.einsum(
            "tyg,ygl->tyl", block_of_queries, lower_state_part, preferred_element_type=jnp.float32
        )
        total_upper, total_lower = split_pair(key_total)
        denominator = jnp.sum(scores.astype(jnp.float32), axis=2).T
        denominator = denominator + jnp.einsum(
            "qhm,hm->qh", block_of_queries, total_upper, preferred_element_type=jnp.float32
        )
        denominator = denominator + jnp.einsum(
            "qhm,hm->qh", block_of_queries, total_lower, preferred_element_type=jnp.float32
        )
        attended_output = (numerator / denominator[:, :, None]).astype(jnp.bfloat16)
        return ((running_state_sum + block_state, key_total + block_total), attended_output)

    pieces = (
        query_map.reshape(block_count, block_rows, head_count, M),
        key_map.reshape(block_count, block_rows, head_count, M),
        values.reshape(block_count, block_rows, head_count, DH),
        states,
        totals,
    )
    finals, output_list = lax.scan(advance, (prior_state, prior_total), pieces)
    return output_list.reshape(length, head_count * DH)


def add_pair(preceding_part, latter):
    return (preceding_part[0] + latter[0], preceding_part[1] + latter[1])


def per_device(projected, conv_filter, frequencies):
    row_count = projected.shape[1]
    rim_rows = KC - 1
    group_size = lax.axis_size("head")
    group_heads = H // group_size
    head_start = lax.axis_index("head") * group_heads
    group_omega = lax.dynamic_slice_in_dim(frequencies, head_start, group_heads, 0)
    before_rim = passed_along(projected[:, row_count - rim_rows :, :], ("ctx", "head"), 1)
    source = convolve(jnp.concatenate([before_rim, projected], axis=1), conv_filter, row_count)
    moved = lax.all_to_all(source, "head", split_axis=2, concat_axis=1, tiled=True)
    query_map, key_map, values = feature_maps(moved, group_omega, group_heads)
    states, totals = block_sums(key_map, values, BLOCK)
    identity = (
        jnp.zeros((group_heads, M, DH), jnp.float32),
        jnp.zeros((group_heads, M), jnp.float32),
    )
    prior_state, prior_total = prefix(
        (jnp.sum(states, axis=0), jnp.sum(totals, axis=0)), "ctx", add_pair, identity
    )
    output_list = attend(
        query_map, key_map, values, states, totals, prior_state, prior_total, BLOCK
    )
    return lax.all_to_all(output_list, "head", split_axis=0, concat_axis=1, tiled=True)


def solution(mesh):
    placed = (P(None, ("ctx", "head"), None), P(), P())
    return jax.shard_map(
        per_device, mesh=mesh, in_specs=placed, out_specs=P(("ctx", "head"), None), check_vma=False
    )
```

profile of v0, /device:TPU:29, one launch (start us, length us, event | category | flops | bytes accessed | tf_op | source)
XLA Modules:
  0.0 265.2 jit_solution(10950722034101237313)
XLA Ops:
  7.7 3.6 %collective-permute-start = (bf16[3,3,4096]{2,1,0:T(4,128)(2,1)S(1)}, bf16[3,3,4096]{2,1,0:T(4,128)(2,1)S(1)}, u32[]{:S(2)}, u32[]{:S(2)}) collective-permute-start(bf16[3,3,4096]{2,1,0:T(4,128)(2,1)S(1)} %slice.39), channel_id=1, source_target_pairs={{0,1},{1,2},{2,3},{3,4},{4,5},{5,6},{6,7},{7,8},{8,9},{9,10},{10,1... | collective-permute-start | bytes 221192 | tf_op jit(solution)/shard_map/ppermute | solution.py:16
  11.3 1.4 fusion.27
  12.7 7.2 %copy.77 = bf16[3,128,4096]{1,0,2:T(4,128)(2,1)} copy(bf16[3,128,4096]{2,1,0:T(8,128)(2,1)} %param.5) | data formatting | bytes 6291456 | tf_op args[0]
  19.9 1.9 copy.112
  21.9 2.0 copy.113
  23.9 2.0 copy.114
  25.9 2.0 copy.115
  27.9 7.5 %fusion.3 = (bf16[3,128,4096]{2,1,0:T(8,128)(2,1)}, bf16[3,128,4096]{2,1,0:T(8,128)(2,1)}, bf16[3,128,4096]{2,1,0:T(8,128)(2,1)}) fusion(bf16[3,3,4096]{2,1,0:T(4,128)(2,1)S(1)} %collective-permute-done, bf16[3,128,4096]{2,1,0:T(8,128)(2,1)} %param.5), kind=kLoop, calls=%fused_computation.12 | loop fusion | flops 18874368 | bytes 12656640 | tf_op jit(solution)/shard_map/concatenate | solution.py:140
  35.4 7.2 %copy.119 = bf16[3,128,4096]{1,0,2:T(4,128)(2,1)} copy(bf16[3,128,4096]{2,1,0:T(8,128)(2,1)} %get-tuple-element.83) | data formatting | bytes 6291456
  42.6 7.2 %copy.120 = bf16[3,128,4096]{1,0,2:T(4,128)(2,1)} copy(bf16[3,128,4096]{2,1,0:T(8,128)(2,1)} %get-tuple-element.85) | data formatting | bytes 6291456
  49.8 7.2 %copy.121 = bf16[3,128,4096]{1,0,2:T(4,128)(2,1)} copy(bf16[3,128,4096]{2,1,0:T(8,128)(2,1)} %get-tuple-element.84) | data formatting | bytes 6291456
  57.0 23.1 %add_convert_fusion = bf16[3,128,4096]{1,0,2:T(4,128)(2,1)} fusion(bf16[3,128,4096]{1,0,2:T(4,128)(2,1)} %copy.121, bf16[3,128,4096]{1,0,2:T(4,128)(2,1)} %copy.120, bf16[3,128,4096]{1,0,2:T(4,128)(2,1)} %copy.119, bf16[3,128,4096]{1,0,2:T(4,128)(2,1)} %copy.77, f32[3,4096]{0,1:T(8,128)} %bitcast.83, f32[3,4096]{0,1:T(8,128)} %bitcast.82, ...), kind=kLoop, calls=%fused_computation.4 | loop fusion | flops 18874368 | bytes 15925248 | tf_op jit(solution)/shard_map/convert_element_type | solution.py:44
  80.1 4.9 %all-to-all-start = ((bf16[3,128,4096]{1,0,2:T(4,128)(2,1)}), bf16[3,128,4096]{1,0,2:T(4,128)(2,1)}, u32[]{:S(2)}, u32[]{:S(2)}) async-start(bf16[3,128,4096]{1,0,2:T(4,128)(2,1)} %add_convert_fusion), calls=%async_computation | async-start | bytes 8388608 | tf_op jit(solution)/shard_map/all_to_all | solution.py:141
  85.0 45.5 %all-to-all-done = bf16[3,128,4096]{1,0,2:T(4,128)(2,1)} async-done(((bf16[3,128,4096]{1,0,2:T(4,128)(2,1)}), bf16[3,128,4096]{1,0,2:T(4,128)(2,1)}, u32[]{:S(2)}, u32[]{:S(2)}) %all-to-all-start) | async-done | bytes 3145760 | tf_op jit(solution)/shard_map/all_to_all | solution.py:141
  130.5 7.1 %copy.84 = bf16[3,128,4,1024]{3,1,2,0:T(8,128)(2,1)} copy(bf16[3,128,4,1024]{1,0,3,2:T(4,128)(2,1)} %bitcast.6) | data formatting | bytes 6291456 | tf_op jit(solution)/shard_map/all_to_all | solution.py:141
  137.7 3.2 %fusion.26 = (bf16[1,4,128,1024]{3,2,1,0:T(8,128)(2,1)S(1)}, bf16[1,4,128,1024]{3,2,1,0:T(8,128)(2,1)S(1)}, bf16[1,4,128,1024]{3,2,1,0:T(8,128)(2,1)}) fusion(bf16[3,4,128,1024]{3,2,1,0:T(8,128)(2,1)} %bitcast.79), kind=kLoop, calls=%fused_computation.43 | loop fusion | bytes 6291456 | tf_op jit(solution)/shard_map/slice | solution.py:63
  142.9 1.3 copy.123
  144.2 1.6 copy.116
  145.8 2.5 fusion.28
  148.3 1.3 copy-done.5
  149.6 1.6 convolution_convert_fusion
  151.3 1.6 copy.124
  153.0 22.1 %all-gather.1 = bf16[64,256]{1,0:T(8,128)(2,1)S(1)} all-gather(bf16[8,256]{1,0:T(8,128)(2,1)S(1)} %get-tuple-element.93), channel_id=3, replica_groups=mesh['ctx'=8,'head'=4] {'ctx'}, dimensions={0}, use_global_device_ids=true | all-gather | bytes 36864 | tf_op jit(solution)/shard_map/all_gather | solution.py:22
  176.0 1.6 convert_reduce_fusion
  177.6 2.1 fusion.29
  179.7 44.7 %all-gather.4.cloned.1.call-done = bf16[64,256,128]{2,1,0:T(8,128)(2,1)} async-done(((bf16[8,256,128]{2,1,0:T(8,128)(2,1)}), bf16[64,256,128]{2,1,0:T(8,128)(2,1)}) %all-gather.4.cloned.1.call-update) | async-done | bytes 4194320 | tf_op jit(solution)/shard_map/all_gather | solution.py:22
  224.4 7.9 %while.2 = (s32[]{:T(128)}, f32[8,256,128]{2,1,0:T(8,128)S(1)}, f32[8,256]{1,0:T(8,128)S(1)}, s32[]{:T(128)}, bf16[8,8,256,128]{3,2,1,0:T(8,128)(2,1)}, /*index=...) while((s32[]{:T(128)}, f32[8,256,128]{2,1,0:T(8,128)S(1)}, f32[8,256]{1,0:T(8,128)S(1)}, ...), condition=%wide.region_3.0_spmd, body=%wide.region_2.0_spmd.sunk | while | flops 528389 | bytes 2642055 | solution.py:36
  232.4 2.1 fusion.7
  234.5 2.0 fusion.5
  238.2 1.6 fusion.4
  239.8 1.3 all_to_all.28
  241.3 15.8 %all_to_all.34 = bf16[4,128,1024]{1,2,0:T(8,128)(2,1)S(1)} all-to-all(bf16[4,128,1024]{1,2,0:T(8,128)(2,1)S(1)} %copy.98), channel_id=1, replica_groups=mesh['ctx'=8,'head'=4] {'head'}, dimensions={0} | all-to-all | bytes 2097152 | tf_op jit(solution)/shard_map/all_to_all | solution.py:154
  (44 shorter events, 15.1 us)
Async XLA Ops:
  6.5 139.3 %copy-start = (bf16[32,128,256]{2,1,0:T(8,128)(2,1)S(1)}, bf16[32,128,256]{2,1,0:T(8,128)(2,1)}, u32[]{:S(2)}) copy-start(bf16[32,128,256]{2,1,0:T(8,128)(2,1)} %param.7) | copy-start | bytes 6291460
  7.7 20.2 %collective-permute-start = (bf16[3,3,4096]{2,1,0:T(4,128)(2,1)S(1)}, bf16[3,3,4096]{2,1,0:T(4,128)(2,1)S(1)}, u32[]{:S(2)}, u32[]{:S(2)}) collective-permute-start(bf16[3,3,4096]{2,1,0:T(4,128)(2,1)S(1)} %slice.39), channel_id=1, source_target_pairs={{0,1},{1,2},{2,3},{3,4},{4,5},{5,6},{6,7},{7,8},{8,9},{9,10},{10,1... | collective-permute-start | bytes 221192 | tf_op jit(solution)/shard_map/ppermute | solution.py:16
  80.1 50.4 %all-to-all-start = ((bf16[3,128,4096]{1,0,2:T(4,128)(2,1)}), bf16[3,128,4096]{1,0,2:T(4,128)(2,1)}, u32[]{:S(2)}, u32[]{:S(2)}) async-start(bf16[3,128,4096]{1,0,2:T(4,128)(2,1)} %add_convert_fusion), calls=%async_computation | async-start | bytes 8388608 | tf_op jit(solution)/shard_map/all_to_all | solution.py:141
  85.0 139.4 %all-gather.4.cloned.1.call-start = ((), (), s32[]{:S(2)}) async-start(), calls=%async_computation.2 | async-start | bytes 4718592 | tf_op jit(solution)/shard_map/all_gather | solution.py:22
  141.2 1.0 copy-start.3
  148.3 1.3 copy-start.5
  151.2 24.7 %copy-start.6 = (bf16[512,8,256]{0,2,1:T(8,128)(2,1)S(1)}, bf16[512,8,256]{0,2,1:T(8,128)(2,1)}, u32[]{:S(2)}) copy-start(bf16[512,8,256]{0,2,1:T(8,128)(2,1)} %copy-done.5) | copy-start | bytes 6291460
  176.0 1.6 copy-start.1
  232.4 4.2 %copy-start.2 = (bf16[8,256,512]{2,1,0:T(8,128)(2,1)S(1)}, bf16[8,256,512]{2,1,0:T(8,128)(2,1)}, u32[]{:S(2)}) copy-start(bf16[8,256,512]{2,1,0:T(8,128)(2,1)} %copy-done.1) | copy-start | bytes 6291460
  236.6 1.6 copy-start.4
Sparse Core Ops, SparseCore 0:
  151.3 72.9 all-gather.3
where the time goes:
time: 268 us; the launch traced here: 265 us
  waiting for transfers between devices  90.2 us (34%)
  local copies, waits for them, and re-layouts  60.8 us (23%)
  other arithmetic  39.2 us (15%)
  blocking collectives  37.9 us (14%)
  matrix products  14.8 us (6%)
  between operations  13.6 us (5%)
  starting transfers between devices  8.52 us (3%)
    all_to_all x1, waiting for transfers between devices, per_device(): lax.all_to_all(source, 'head', split_axis=2, concat_axis=1, tiled=True)  45.5 us
    all_gather x1, waiting for transfers between devices, prefix(): lax.all_gather(a.astype(kind), axis)  44.7 us
    unnamed x21, local copies, waits for them, and re-layouts  35.3 us
    convert_element_type x1, other arithmetic, convolve(): return summed.astype(jnp.bfloat16)  23.1 us
    all_gather x1, blocking collectives, prefix(): lax.all_gather(a.astype(kind), axis)  22.1 us
    all_to_all x1, blocking collectives, per_device(): lax.all_to_all(output_list, 'head', split_axis=0, concat_axis=1, tiled=True)  15.8 us
    mul x4, local copies, waits for them, and re-layouts, convolve(): conv_taps[:, offset][:, None, :] * window.astype(jnp.float32)  7.95 us
    add x12, other arithmetic, add_pair(): return (preceding_part[0] + latter[0], preceding_part[1] + latter[1])  7.73 us
  transfers between devices with their start and end apart: 3, of which 2 were waited for; matrix products, arithmetic and copies ran while one was open for 9% of the time, Pallas kernels for 0%

commit v1 on v0

v1 whole, which is shorter than its diff:
```python
import functools

import jax
import jax.numpy as jnp
from jax import lax
from jax.experimental import pallas as pl
from jax.experimental.pallas import tpu as pltpu
from jax.sharding import PartitionSpec as P

DH = 128
M = 256
KC = 4
CORES = 2
RIM = 16
SROWS = DH + 16
MESH = pl.DeviceIdType.MESH


def kernel(
    plan,
    proj, filt, freq, out,
    x_all, omega, kf, vals, qf, intra, s_send, s_recv, chain_in, chain_out, r_send, r_recv, outb,
    load_sem, freq_sem, ex_send, ex_recv, rim_send, rim_recv,
    ss_sem, sr_sem, cs_sem, cr_sem, rs_sem, rr_sem, os_sem, or_sem, ol_sem,
):
    X, Y, Z = plan
    G = X * Y
    rows = proj.shape[1]
    half = proj.shape[2] // CORES
    J = half // DH // G
    T = CORES * rows
    wide = G * DH
    scale = DH ** (-0.25)

    c = lax.axis_index("ctx")
    hd = lax.axis_index("head")
    y, core = hd // CORES, hd % CORES
    z, x = c // X, c % X
    me = x * Y + y
    other = 1 - core
    chip = c * Y + y
    chips = X * Y * Z

    def member(g):
        return (z * X + g // Y, (g % Y) * CORES + core)

    def at_chip(n, k):
        return (n // Y, (n % Y) * CORES + k)

    mate = (c, y * CORES + other)
    has_next = (core == 1) & (chip < chips - 1)
    has_prev = chip > 0

    barrier = pltpu.get_barrier_semaphore()

    def greet(dev):
        pl.semaphore_signal(barrier, inc=1, device_id=dev, device_id_type=MESH)

    greet(mate)
    for g in range(G):
        pl.when(g != me)(lambda g=g: greet(member(g)))
    pl.when(z > 0)(lambda: greet((c - X, hd)))
    pl.when(z < Z - 1)(lambda: greet((c + X, hd)))
    for k in range(CORES):
        pl.when(has_next)(lambda k=k: greet(at_chip(chip + 1, k)))
    pl.when(has_prev)(lambda: greet(at_chip(chip - 1, 1)))

    my_cols = pl.ds(pl.multiple_of(core * half, half), half)
    mate_cols = pl.ds(pl.multiple_of(other * half, half), half)
    my_rows = pl.ds(pl.multiple_of(RIM + core * rows, 16), rows)
    mate_rows = pl.ds(pl.multiple_of(RIM + other * rows, 16), rows)

    def load(a):
        return pltpu.make_async_copy(
            proj.at[a, :, my_cols], x_all.at[a, my_rows, :], load_sem.at[a]
        )

    def exchange(a):
        return pltpu.make_async_remote_copy(
            proj.at[a, :, mate_cols], x_all.at[a, my_rows, :],
            ex_send.at[a], ex_recv.at[a], device_id=mate, device_id_type=MESH,
        )

    def rim(a, k):
        return pltpu.make_async_remote_copy(
            proj.at[a, pl.ds(rows - RIM, RIM), pl.ds(k * half, half)],
            x_all.at[a, pl.ds(0, RIM), :],
            rim_send.at[a, k], rim_recv.at[a],
            device_id=at_chip(chip + 1, k), device_id_type=MESH,
        )

    omega_copy = pltpu.make_async_copy(
        freq.at[pl.ds(core * (half // DH), half // DH)], omega, freq_sem
    )
    for a in (1, 2, 0):
        load(a).start()
    omega_copy.start()

    @pl.when(jnp.logical_not(has_prev))
    def _():
        x_all[:, pl.ds(0, RIM), :] = jnp.zeros((3, RIM, half), x_all.dtype)

    greeted = (
        G + (z > 0).astype(jnp.int32) + (z < Z - 1).astype(jnp.int32)
        + CORES * has_next.astype(jnp.int32) + has_prev.astype(jnp.int32)
    )
    pl.semaphore_wait(barrier, greeted)

    for a in (1, 2, 0):
        for k in range(CORES):
            pl.when(has_next)(lambda a=a, k=k: rim(a, k).start())
        exchange(a).start()

    def arrive(a):
        load(a).wait()
        exchange(a).wait_recv()

        @pl.when(has_prev)
        def _():
            pltpu.make_async_copy(
                x_all.at[a, pl.ds(0, RIM), :], x_all.at[a, pl.ds(0, RIM), :], rim_recv.at[a]
            ).wait()

    def conv(a, h):
        cols = pl.ds(pl.multiple_of(h * DH, DH), DH)
        taps = filt[a, :, pl.ds(pl.multiple_of(core * half + h * DH, DH), DH)]
        data = x_all[a, :, cols].astype(jnp.float32)
        total = taps[0:1] * data[RIM:]
        for j in range(1, KC):
            total = total + taps[j : j + 1] * pltpu.roll(data, j, 0)[RIM:]
        return total.astype(jnp.bfloat16)

    def s_copy(j, o):
        return pltpu.make_async_remote_copy(
            s_send.at[j, o], s_recv.at[j, me], ss_sem.at[j, o], sr_sem.at[j, me],
            device_id=member(o), device_id_type=MESH,
        )

    def s_arrival(j, g):
        return pltpu.make_async_remote_copy(
            s_send.at[j, g], s_recv.at[j, g], ss_sem.at[j, g], sr_sem.at[j, g],
            device_id=member(g), device_id_type=MESH,
        )

    def r_copy(j, g):
        return pltpu.make_async_remote_copy(
            r_send.at[j, g], r_recv.at[j, me], rs_sem.at[j, g], rr_sem.at[j, me],
            device_id=member(g), device_id_type=MESH,
        )

    def r_arrival(j, o):
        return pltpu.make_async_remote_copy(
            r_send.at[j, o], r_recv.at[j, o], rs_sem.at[j, o], rr_sem.at[j, o],
            device_id=member(o), device_id_type=MESH,
        )

    def chain(j):
        return pltpu.make_async_remote_copy(
            chain_out.at[j], chain_in.at[j], cs_sem.at[j], cr_sem.at[j],
            device_id=(c + X, hd), device_id_type=MESH,
        )

    def keys_and_sums(j, o):
        h = j * G + o
        k = conv(1, h)
        v = conv(2, h)
        wide_k = k.astype(jnp.float32)
        norm = jnp.sum(wide_k * wide_k, axis=1, keepdims=True) * (0.5 * scale * scale)
        part = jnp.dot(k, omega[h], preferred_element_type=jnp.float32)
        feats = jnp.exp(part * scale - norm).astype(jnp.bfloat16)
        kf[h] = feats
        vals[h] = v
        joined = jnp.concatenate([v, jnp.ones_like(v)], axis=1)
        sums = lax.dot_general(
            joined, feats, (((0,), (0,)), ((), ())), preferred_element_type=jnp.float32
        )
        sums = sums[:SROWS].astype(jnp.bfloat16)

        @pl.when(o == me)
        def _():
            s_recv[j, o] = sums

        @pl.when(o != me)
        def _():
            s_send[j, o] = sums
            s_copy(j, o).start()

    def own(j):
        def await_sums(g, _):
            pl.when(g != me)(lambda: s_arrival(j, g).wait_recv())
            return 0

        lax.fori_loop(0, G, await_sums, 0)
        total = s_recv[j, 0].astype(jnp.float32)
        for g in range(1, G):
            total = total + s_recv[j, g].astype(jnp.float32)

        @pl.when(z == 0)
        def _():
            chain_in[j] = jnp.zeros((SROWS, M), jnp.bfloat16)

        @pl.when(z > 0)
        def _():
            chain(j).wait_recv()

        before = chain_in[j].astype(jnp.float32)

        @pl.when(z < Z - 1)
        def _():
            chain_out[j] = (before + total).astype(jnp.bfloat16)
            chain(j).start()

        running = before
        for g in range(G):
            piece = running.astype(jnp.bfloat16)

            @pl.when(g == me)
            def _():
                r_recv[j, g] = piece

            @pl.when(g != me)
            def _():
                r_send[j, g] = piece
                r_copy(j, g).start()

            if g < G - 1:
                running = running + s_recv[j, g].astype(jnp.float32)

    def within(j, o):
        h = j * G + o
        q = conv(0, h)
        part = jnp.dot(q, omega[h], preferred_element_type=jnp.float32)
        feats = jnp.exp(part * scale).astype(jnp.bfloat16)
        qf[h] = feats
        scores = lax.dot_general(
            feats, kf[h], (((1,), (1,)), ((), ())), preferred_element_type=jnp.float32
        )
        at = lax.broadcasted_iota(jnp.int32, (T, T), 0)
        of = lax.broadcasted_iota(jnp.int32, (T, T), 1)
        scores = jnp.where(at >= of, scores, 0.0).astype(jnp.bfloat16)
        v = vals[h]
        joined = jnp.concatenate([v, jnp.ones_like(v)], axis=1)
        intra[h] = jnp.dot(scores, joined, preferred_element_type=jnp.float32)

    def finish(j, o):
        h = j * G + o
        pl.when(o != me)(lambda: r_arrival(j, o).wait_recv())
        state = r_recv[j, o]
        joined = jnp.concatenate([state[:DH]] + [state[DH:]] * (DH // 16), axis=0)
        both = intra[h] + lax.dot_general(
            qf[h], joined, (((1,), (1,)), ((), ())), preferred_element_type=jnp.float32
        )
        result = (both[:, :DH] / both[:, DH:]).astype(jnp.bfloat16)
        outb[:, pl.ds(pl.multiple_of(h * DH, DH), DH)] = result

    def out_cols(j):
        return pl.ds(pl.multiple_of(j * wide, wide), wide)

    def out_remote(j):
        return pltpu.make_async_remote_copy(
            outb.at[pl.ds(pl.multiple_of(other * rows, rows), rows), out_cols(j)],
            out.at[:, pl.ds(pl.multiple_of(core * half + j * wide, wide), wide)],
            os_sem.at[j], or_sem.at[j], device_id=mate, device_id_type=MESH,
        )

    def out_local(j):
        return pltpu.make_async_copy(
            outb.at[pl.ds(pl.multiple_of(core * rows, rows), rows), out_cols(j)],
            out.at[:, pl.ds(pl.multiple_of(core * half + j * wide, wide), wide)],
            ol_sem.at[j],
        )

    def over(count, body):
        def step(i, _):
            body(i)
            return 0

        lax.fori_loop(0, count, step, 0)

    omega_copy.wait()
    arrive(1)
    arrive(2)
    over(J, lambda j: over(G, lambda o: keys_and_sums(j, o)))
    arrive(0)

    def middle(j):
        own(j)
        over(G, lambda o: within(j, o))

    over(J, middle)

    def last(j):
        over(G, lambda o: finish(j, o))
        out_remote(j).start()
        out_local(j).start()

    over(J, last)

    for a in range(3):
        exchange(a).wait_send()
        for k in range(CORES):
            pl.when(has_next)(lambda a=a, k=k: rim(a, k).wait_send())

    def drain(j):
        def one(g):
            @pl.when(g != me)
            def _():
                s_copy(j, g).wait_send()
                r_copy(j, g).wait_send()

        over(G, one)
        pl.when(z < Z - 1)(lambda: chain(j).wait_send())
        out_remote(j).wait()
        out_local(j).wait()

    over(J, drain)


def plan_of(ctx_size, head_size):
    along_x = 1
    while along_x * along_x * 4 <= ctx_size:
        along_x *= 2
    return along_x, head_size // CORES, ctx_size // along_x


def per_device(projected, conv_filter, frequencies):
    plan = plan_of(lax.axis_size("ctx"), lax.axis_size("head"))
    rows, width = projected.shape[1], projected.shape[2]
    half = width // CORES
    heads = half // DH
    group = plan[0] * plan[1]
    slots = heads // group
    T = CORES * rows
    bf16 = jnp.bfloat16
    dma = pltpu.SemaphoreType.DMA
    return pl.pallas_call(
        functools.partial(kernel, plan),
        out_shape=jax.ShapeDtypeStruct((rows, width), bf16),
        in_specs=[
            pl.BlockSpec(memory_space=pl.ANY),
            pl.BlockSpec(memory_space=pltpu.VMEM),
            pl.BlockSpec(memory_space=pl.ANY),
        ],
        out_specs=pl.BlockSpec(memory_space=pl.ANY),
        scratch_shapes=[
            pltpu.VMEM((3, RIM + T, half), bf16),
            pltpu.VMEM((heads, DH, M), bf16),
            pltpu.VMEM((heads, T, M), bf16),
            pltpu.VMEM((heads, T, DH), bf16),
            pltpu.VMEM((heads, T, M), bf16),
            pltpu.VMEM((heads, T, 2 * DH), jnp.float32),
            pltpu.VMEM((slots, group, SROWS, M), bf16),
            pltpu.VMEM((slots, group, SROWS, M), bf16),
            pltpu.VMEM((slots, SROWS, M), bf16),
            pltpu.VMEM((slots, SROWS, M), bf16),
            pltpu.VMEM((slots, group, SROWS, M), bf16),
            pltpu.VMEM((slots, group, SROWS, M), bf16),
            pltpu.VMEM((T, half), bf16),
            dma((3,)), dma, dma((3,)), dma((3,)), dma((3, CORES)), dma((3,)),
            dma((slots, group)), dma((slots, group)),
            dma((slots,)), dma((slots,)),
            dma((slots, group)), dma((slots, group)),
            dma((slots,)), dma((slots,)), dma((slots,)),
        ],
        compiler_params=pltpu.CompilerParams(
            collective_id=0, has_side_effects=True, vmem_limit_bytes=48 * 1024 * 1024
        ),
        cost_estimate=pl.CostEstimate(
            flops=2_000_000_000, bytes_accessed=8_000_000, transcendentals=2_000_000
        ),
    )(projected, conv_filter, frequencies)


def solution(mesh):
    placed = (P(None, ("ctx", "head"), None), P(), P())
    return jax.shard_map(
        per_device, mesh=mesh, in_specs=placed, out_specs=P(("ctx", "head"), None), check_vma=False
    )
```

time: 268 us -> 42.9 us (0.16)
  waiting for transfers between devices: 90.2 us -> 0 us
  local copies, waits for them, and re-layouts: 60.8 us -> 3.49 us
  other arithmetic: 39.2 us -> 0 us
  Pallas kernels: 0 us -> 39.1 us
  blocking collectives: 37.9 us -> 0 us
  matrix products: 14.8 us -> 0 us
  between operations: 13.6 us -> 0.01 us
  starting transfers between devices: 8.52 us -> 0 us
    all_to_all x1 -> x0, waiting for transfers between devices: 45.5 us -> none  [per_device(): lax.all_to_all(source, 'head', split_axis=2, concat_axis=1, tiled=True)]
    all_gather x1 -> x0, waiting for transfers between devices: 44.7 us -> none  [prefix(): lax.all_gather(a.astype(kind), axis)]
    pallas_call x0 -> x1, Pallas kernels: none -> 39.1 us  [per_device(): pl.pallas_call(functools.partial(kernel, plan), out_shape=jax.ShapeDtypeS...]
    unnamed x21 -> x5, local copies, waits for them, and re-layouts: 35.3 us -> 3.49 us
    convert_element_type x4 -> x0, other arithmetic: 23.2 us -> none  [the longest x1 23.1 us: convolve(): return summed.astype(jnp.bfloat16)]
    all_gather x1 -> x0, blocking collectives: 22.1 us -> none  [prefix(): lax.all_gather(a.astype(kind), axis)]
    all_to_all x1 -> x0, blocking collectives: 15.8 us -> none  [per_device(): lax.all_to_all(output_list, 'head', split_axis=0, concat_axis=1, tiled=True)]
    dot_general x9 -> x0, matrix products: 14.8 us -> none  [the longest x1 2.47 us: feature_maps(): jnp.einsum('lhd,hdm->lhm', per_head[1], head_omega, preferred_element_typ...]
  transfers between devices with their start and end apart: 3 -> 0, of which waited for: 2 -> 0; matrix products, arithmetic and copies ran while one was open for 9% -> 0% of each run, Pallas kernels for 0% -> 0%
where the time goes in v1:
time: 42.9 us; the launch traced here: 42.6 us
  Pallas kernels  39.1 us (91%)
  local copies, waits for them, and re-layouts  3.49 us (8%)
    pallas_call x1, Pallas kernels, per_device(): pl.pallas_call(functools.partial(kernel, plan), out_shape=jax.ShapeDtypeS...  39.1 us
    unnamed x5, local copies, waits for them, and re-layouts  3.49 us

profile of v1, /device:TPU:29, one launch (start us, length us, event | category | flops | bytes accessed | tf_op | source)
XLA Modules:
  0.0 42.6 jit_solution(8460737720920095180)
XLA Ops:
  0.0 0.0 copy-start
  0.0 1.6 %copy-done = bf16[32,128,256]{2,1,0:T(8,128)(2,1)S(1)} copy-done((bf16[32,128,256]{2,1,0:T(8,128)(2,1)S(1)}, bf16[32,128,256]{2,1,0:T(8,128)(2,1)}, u32[]{:S(2)}) %copy-start) | copy-done | bytes 2097176
  1.6 0.0 copy-start.1
  1.6 0.9 %copy-done.1 = f32[3,4,4096]{2,1,0:T(4,128)S(1)} copy-done((f32[3,4,4096]{2,1,0:T(4,128)S(1)}, f32[3,4,4096]{2,1,0:T(4,128)}, u32[]{:S(2)}) %copy-start.1) | copy-done | bytes 196632
  2.5 39.1 %shard_map.37 = bf16[128,4096]{1,0:T(8,128)(2,1)S(1)} custom-call(bf16[3,128,4096]{2,1,0:T(8,128)(2,1)} %proj.1, f32[3,4,4096]{2,1,0:T(4,128)S(1)} %copy-done.1, bf16[32,128,256]{2,1,0:T(8,128)(2,1)S(1)} %copy-done), custom_call_target="tpu_custom_call" | custom-call | flops 2000000000 | bytes 8000000 | tf_op jit(solution)/shard_map/pallas_call | solution.py:336
  41.6 1.0 %copy.5 = bf16[128,4096]{1,0:T(8,128)(2,1)} copy(bf16[128,4096]{1,0:T(8,128)(2,1)S(1)} %shard_map.37) | data formatting | bytes 2097152
Async XLA Ops:
  0.0 1.6 %copy-start = (bf16[32,128,256]{2,1,0:T(8,128)(2,1)S(1)}, bf16[32,128,256]{2,1,0:T(8,128)(2,1)}, u32[]{:S(2)}) copy-start(bf16[32,128,256]{2,1,0:T(8,128)(2,1)} %freq.1) | copy-start | bytes 6291460
  1.6 0.9 %copy-start.1 = (f32[3,4,4096]{2,1,0:T(4,128)S(1)}, f32[3,4,4096]{2,1,0:T(4,128)}, u32[]{:S(2)}) copy-start(f32[3,4,4096]{2,1,0:T(4,128)} %filt.1) | copy-start | bytes 589828

commit v2 on v1

--- a/solution.py
+++ b/solution.py
@@ -12,15 +12,15 @@
 KC = 4
 CORES = 2
 RIM = 16
-SROWS = DH + 16
+SROWS = 2 * DH + 16
 MESH = pl.DeviceIdType.MESH
 
 
 def kernel(
     plan,
     proj, filt, freq, out,
-    x_all, omega, kf, vals, qf, intra, s_send, s_recv, chain_in, chain_out, r_send, r_recv, outb,
-    load_sem, freq_sem, ex_send, ex_recv, rim_send, rim_recv,
+    x_all, tail, packed, rim_in, taps_all, omega, kf, vals, qf, intra, s_send, s_recv, chain_in, chain_out, r_send, r_recv, outb,
+    load_sem, freq_sem, filt_sem, tail_sem, ex_send, ex_recv, rim_send, rim_recv,
     ss_sem, sr_sem, cs_sem, cr_sem, rs_sem, rr_sem, os_sem, or_sem, ol_sem,
 ):
     X, Y, Z = plan
@@ -66,39 +66,54 @@
     pl.when(has_prev)(lambda: greet(at_chip(chip - 1, 1)))
 
     my_cols = pl.ds(pl.multiple_of(core * half, half), half)
-    mate_cols = pl.ds(pl.multiple_of(other * half, half), half)
     my_rows = pl.ds(pl.multiple_of(RIM + core * rows, 16), rows)
-    mate_rows = pl.ds(pl.multiple_of(RIM + other * rows, 16), rows)
 
     def load(a):
         return pltpu.make_async_copy(
             proj.at[a, :, my_cols], x_all.at[a, my_rows, :], load_sem.at[a]
         )
 
-    def exchange(a):
-        return pltpu.make_async_remote_copy(
-            proj.at[a, :, mate_cols], x_all.at[a, my_rows, :],
-            ex_send.at[a], ex_recv.at[a], device_id=mate, device_id_type=MESH,
-        )
-
-    def rim(a, k):
-        return pltpu.make_async_remote_copy(
-            proj.at[a, pl.ds(rows - RIM, RIM), pl.ds(k * half, half)],
-            x_all.at[a, pl.ds(0, RIM), :],
-            rim_send.at[a, k], rim_recv.at[a],
+    def exchange(a, j):
+        far = pl.ds(pl.multiple_of(other * half + j * wide, wide), wide)
+        near = pl.ds(pl.multiple_of(j * wide, wide), wide)
+        return pltpu.make_async_remote_copy(
+            proj.at[a, :, far], x_all.at[a, my_rows, near],
+            ex_send.at[a, j], ex_recv.at[a, j], device_id=mate, device_id_type=MESH,
+        )
+
+    def rim(k):
+        return pltpu.make_async_remote_copy(
+            packed.at[:, pl.ds(k * half, half)], rim_in,
+            rim_send.at[k], rim_recv,
             device_id=at_chip(chip + 1, k), device_id_type=MESH,
         )
+
+    tail_copy = pltpu.make_async_copy(proj.at[:, pl.ds(rows - RIM, RIM), :], tail, tail_sem)
+    taps_copy = pltpu.make_async_copy(filt.at[:, :, my_cols], taps_all, filt_sem)
 
     omega_copy = pltpu.make_async_copy(
         freq.at[pl.ds(core * (half // DH), half // DH)], omega, freq_sem
     )
-    for a in (1, 2, 0):
-        load(a).start()
+    pl.when(has_next)(tail_copy.start)
+    load(1).start()
+    load(2).start()
+    taps_copy.start()
     omega_copy.start()
+    load(0).start()
+
+    @pl.when(has_next)
+    def _():
+        tail_copy.wait()
+        row = lax.broadcasted_iota(jnp.int32, (RIM, half), 0)
+        for k in range(CORES):
+            parts = [tail[a, :, pl.ds(k * half, half)].astype(jnp.float32) for a in range(3)]
+            both = jnp.where(row >= RIM - 6, pltpu.roll(parts[1], RIM - 3, 0), pltpu.roll(parts[2], RIM - 6, 0))
+            joined = jnp.where(row >= RIM - 3, parts[0], both)
+            packed[:, pl.ds(k * half, half)] = joined.astype(packed.dtype)
 
     @pl.when(jnp.logical_not(has_prev))
     def _():
-        x_all[:, pl.ds(0, RIM), :] = jnp.zeros((3, RIM, half), x_all.dtype)
+        rim_in[...] = jnp.zeros((RIM, half), rim_in.dtype)
 
     greeted = (
         G + (z > 0).astype(jnp.int32) + (z < Z - 1).astype(jnp.int32)
@@ -106,24 +121,17 @@
     )
     pl.semaphore_wait(barrier, greeted)
 
-    for a in (1, 2, 0):
-        for k in range(CORES):
-            pl.when(has_next)(lambda a=a, k=k: rim(a, k).start())
-        exchange(a).start()
-
-    def arrive(a):
-        load(a).wait()
-        exchange(a).wait_recv()
-
-        @pl.when(has_prev)
-        def _():
-            pltpu.make_async_copy(
-                x_all.at[a, pl.ds(0, RIM), :], x_all.at[a, pl.ds(0, RIM), :], rim_recv.at[a]
-            ).wait()
+    for k in range(CORES):
+        pl.when(has_next)(lambda k=k: rim(k).start())
+    for j in range(J):
+        exchange(1, j).start()
+        exchange(2, j).start()
+    for j in range(J):
+        exchange(0, j).start()
 
     def conv(a, h):
         cols = pl.ds(pl.multiple_of(h * DH, DH), DH)
-        taps = filt[a, :, pl.ds(pl.multiple_of(core * half + h * DH, DH), DH)]
+        taps = taps_all[a, :, cols]
         data = x_all[a, :, cols].astype(jnp.float32)
         total = taps[0:1] * data[RIM:]
         for j in range(1, KC):
@@ -174,7 +182,9 @@
         sums = lax.dot_general(
             joined, feats, (((0,), (0,)), ((), ())), preferred_element_type=jnp.float32
         )
-        sums = sums[:SROWS].astype(jnp.bfloat16)
+        sums = jnp.concatenate(
+            [sums[:DH, :DH], sums[:DH, DH:], sums[DH : DH + 8, :DH], sums[DH : DH + 8, DH:]], axis=0
+        ).astype(jnp.bfloat16)
 
         @pl.when(o == me)
         def _():
@@ -197,7 +207,7 @@
 
         @pl.when(z == 0)
         def _():
-            chain_in[j] = jnp.zeros((SROWS, M), jnp.bfloat16)
+            chain_in[j] = jnp.zeros((SROWS, DH), jnp.bfloat16)
 
         @pl.when(z > 0)
         def _():
@@ -246,7 +256,11 @@
         h = j * G + o
         pl.when(o != me)(lambda: r_arrival(j, o).wait_recv())
         state = r_recv[j, o]
-        joined = jnp.concatenate([state[:DH]] + [state[DH:]] * (DH // 16), axis=0)
+        weights = state[2 * DH :].astype(jnp.float32)
+        weights = jnp.concatenate([weights[:8], weights[8:]], axis=1)
+        weights = jnp.concatenate([weights, weights], axis=0).astype(jnp.bfloat16)
+        sums = jnp.concatenate([state[:DH], state[DH : 2 * DH]], axis=1)
+        joined = jnp.concatenate([sums] + [weights] * (DH // 16), axis=0)
         both = intra[h] + lax.dot_general(
             qf[h], joined, (((1,), (1,)), ((), ())), preferred_element_type=jnp.float32
         )
@@ -277,14 +291,30 @@
 
         lax.fori_loop(0, count, step, 0)
 
+    def ordered(i):
+        return lax.rem(x + 1 + i, X) * Y + lax.rem(y + 1 + i // X, Y)
+
+    taps_copy.wait()
     omega_copy.wait()
-    arrive(1)
-    arrive(2)
-    over(J, lambda j: over(G, lambda o: keys_and_sums(j, o)))
-    arrive(0)
+    load(1).wait()
+    load(2).wait()
+    load(0).wait()
+    pl.when(has_prev)(lambda: rim(0).wait_recv())
+    edge = rim_in[...].astype(jnp.float32)
+    for a in range(3):
+        moved = pltpu.roll(edge, 3 * a, 0) if a else edge
+        x_all[a, pl.ds(0, RIM), :] = moved.astype(x_all.dtype)
+
+    def first(j):
+        exchange(1, j).wait_recv()
+        exchange(2, j).wait_recv()
+        over(G, lambda i: keys_and_sums(j, ordered(i)))
+
+    over(J, first)
 
     def middle(j):
         own(j)
+        exchange(0, j).wait_recv()
         over(G, lambda o: within(j, o))
 
     over(J, middle)
@@ -296,12 +326,13 @@
 
     over(J, last)
 
-    for a in range(3):
-        exchange(a).wait_send()
-        for k in range(CORES):
-            pl.when(has_next)(lambda a=a, k=k: rim(a, k).wait_send())
+    for k in range(CORES):
+        pl.when(has_next)(lambda k=k: rim(k).wait_send())
 
     def drain(j):
+        for a in range(3):
+            exchange(a, j).wait_send()
+
         def one(g):
             @pl.when(g != me)
             def _():
@@ -338,32 +369,36 @@
         out_shape=jax.ShapeDtypeStruct((rows, width), bf16),
         in_specs=[
             pl.BlockSpec(memory_space=pl.ANY),
-            pl.BlockSpec(memory_space=pltpu.VMEM),
+            pl.BlockSpec(memory_space=pl.ANY),
             pl.BlockSpec(memory_space=pl.ANY),
         ],
         out_specs=pl.BlockSpec(memory_space=pl.ANY),
         scratch_shapes=[
             pltpu.VMEM((3, RIM + T, half), bf16),
+            pltpu.VMEM((3, RIM, width), bf16),
+            pltpu.VMEM((RIM, width), bf16),
+            pltpu.VMEM((RIM, half), bf16),
+            pltpu.VMEM((3, KC, half), jnp.float32),
             pltpu.VMEM((heads, DH, M), bf16),
             pltpu.VMEM((heads, T, M), bf16),
             pltpu.VMEM((heads, T, DH), bf16),
             pltpu.VMEM((heads, T, M), bf16),
             pltpu.VMEM((heads, T, 2 * DH), jnp.float32),
-            pltpu.VMEM((slots, group, SROWS, M), bf16),
-            pltpu.VMEM((slots, group, SROWS, M), bf16),
-            pltpu.VMEM((slots, SROWS, M), bf16),
-            pltpu.VMEM((slots, SROWS, M), bf16),
-            pltpu.VMEM((slots, group, SROWS, M), bf16),
-            pltpu.VMEM((slots, group, SROWS, M), bf16),
+            pltpu.VMEM((slots, group, SROWS, DH), bf16),
+            pltpu.VMEM((slots, group, SROWS, DH), bf16),
+            pltpu.VMEM((slots, SROWS, DH), bf16),
+            pltpu.VMEM((slots, SROWS, DH), bf16),
+            pltpu.VMEM((slots, group, SROWS, DH), bf16),
+            pltpu.VMEM((slots, group, SROWS, DH), bf16),
             pltpu.VMEM((T, half), bf16),
-            dma((3,)), dma, dma((3,)), dma((3,)), dma((3, CORES)), dma((3,)),
+            dma((3,)), dma, dma, dma, dma((3, slots)), dma((3, slots)), dma((CORES,)), dma,
             dma((slots, group)), dma((slots, group)),
             dma((slots,)), dma((slots,)),
             dma((slots, group)), dma((slots, group)),
             dma((slots,)), dma((slots,)), dma((slots,)),
         ],
         compiler_params=pltpu.CompilerParams(
-            collective_id=0, has_side_effects=True, vmem_limit_bytes=48 * 1024 * 1024
+            collective_id=0, has_side_effects=True, vmem_limit_bytes=60 * 1024 * 1024
         ),
         cost_estimate=pl.CostEstimate(
             flops=2_000_000_000, bytes_accessed=8_000_000, transcendentals=2_000_000

time: 42.9 us -> 39.5 us (0.921)
  Pallas kernels: 39.1 us -> 37.1 us
  local copies, waits for them, and re-layouts: 3.49 us -> 2.29 us
    pallas_call x1, Pallas kernels: 39.1 us -> 37.1 us  [per_device(): pl.pallas_call(functools.partial(kernel, plan), out_shape=jax.ShapeDtypeS...]
    unnamed x5 -> x1, local copies, waits for them, and re-layouts: 3.49 us -> 2.29 us
where the time goes in v2:
time: 39.5 us; the launch traced here: 39.4 us
  Pallas kernels  37.1 us (94%)
  local copies, waits for them, and re-layouts  2.29 us (6%)
    pallas_call x1, Pallas kernels, per_device(): pl.pallas_call(functools.partial(kernel, plan), out_shape=jax.ShapeDtypeS...  37.1 us
    unnamed x1, local copies, waits for them, and re-layouts  2.29 us

profile of v2, /device:TPU:29, one launch (start us, length us, event | category | flops | bytes accessed | tf_op | source)
XLA Modules:
  0.0 39.4 jit_solution(2678469390247569411)
XLA Ops:
  0.0 37.1 %shard_map.37 = bf16[128,4096]{1,0:T(8,128)(2,1)} custom-call(bf16[3,128,4096]{2,1,0:T(8,128)(2,1)} %proj.1, f32[3,4,4096]{2,1,0:T(4,128)} %filt.1, bf16[32,128,256]{2,1,0:T(8,128)(2,1)} %freq.1), custom_call_target="tpu_custom_call" | custom-call | flops 2000000000 | bytes 8000000 | tf_op jit(solution)/shard_map/pallas_call | solution.py:367
  37.1 2.3 %copy.5 = bf16[128,4096]{1,0:T(8,128)(2,1)} copy(bf16[128,4096]{1,0:T(8,128)(2,1)} %shard_map.37) | data formatting | bytes 2097152

commit v3 on v2

--- a/solution.py
+++ b/solution.py
@@ -168,32 +168,33 @@
             device_id=(c + X, hd), device_id_type=MESH,
         )
 
-    def keys_and_sums(j, o):
-        h = j * G + o
-        k = conv(1, h)
-        v = conv(2, h)
-        wide_k = k.astype(jnp.float32)
-        norm = jnp.sum(wide_k * wide_k, axis=1, keepdims=True) * (0.5 * scale * scale)
-        part = jnp.dot(k, omega[h], preferred_element_type=jnp.float32)
-        feats = jnp.exp(part * scale - norm).astype(jnp.bfloat16)
-        kf[h] = feats
-        vals[h] = v
-        joined = jnp.concatenate([v, jnp.ones_like(v)], axis=1)
-        sums = lax.dot_general(
-            joined, feats, (((0,), (0,)), ((), ())), preferred_element_type=jnp.float32
-        )
-        sums = jnp.concatenate(
-            [sums[:DH, :DH], sums[:DH, DH:], sums[DH : DH + 8, :DH], sums[DH : DH + 8, DH:]], axis=0
-        ).astype(jnp.bfloat16)
-
-        @pl.when(o == me)
-        def _():
-            s_recv[j, o] = sums
-
-        @pl.when(o != me)
-        def _():
-            s_send[j, o] = sums
-            s_copy(j, o).start()
+    def keys_and_sums(j, places):
+        heads = [j * G + o for o in places]
+        ks = [conv(1, h) for h in heads]
+        vs = [conv(2, h) for h in heads]
+        parts = [
+            jnp.dot(k, omega[h], preferred_element_type=jnp.float32) for k, h in zip(ks, heads)
+        ]
+        wides = [k.astype(jnp.float32) for k in ks]
+        norms = [
+            jnp.sum(w * w, axis=1, keepdims=True) * (0.5 * scale * scale) for w in wides
+        ]
+        feats = [
+            jnp.exp(part * scale - norm).astype(jnp.bfloat16) for part, norm in zip(parts, norms)
+        ]
+        sums = [
+            lax.dot_general(
+                jnp.concatenate([v, jnp.ones_like(v)], axis=1), f,
+                (((0,), (0,)), ((), ())), preferred_element_type=jnp.float32,
+            )
+            for v, f in zip(vs, feats)
+        ]
+        for h, o, v, f, w in zip(heads, places, vs, feats, sums):
+            kf[h] = f
+            vals[h] = v
+            s_send[j, o] = jnp.concatenate(
+                [w[:DH, :DH], w[:DH, DH:], w[DH : DH + 8, :DH], w[DH : DH + 8, DH:]], axis=0
+            ).astype(jnp.bfloat16)
 
     def own(j):
         def await_sums(g, _):
@@ -236,52 +237,74 @@
             if g < G - 1:
                 running = running + s_recv[j, g].astype(jnp.float32)
 
-    def within(j, o):
-        h = j * G + o
-        q = conv(0, h)
-        part = jnp.dot(q, omega[h], preferred_element_type=jnp.float32)
-        feats = jnp.exp(part * scale).astype(jnp.bfloat16)
-        qf[h] = feats
-        scores = lax.dot_general(
-            feats, kf[h], (((1,), (1,)), ((), ())), preferred_element_type=jnp.float32
-        )
+    def within(heads):
+        qs = [conv(0, h) for h in heads]
+        keys = [kf[h] for h in heads]
+        vs = [vals[h] for h in heads]
+        parts = [
+            jnp.dot(q, omega[h], preferred_element_type=jnp.float32) for q, h in zip(qs, heads)
+        ]
+        feats = [jnp.exp(part * scale).astype(jnp.bfloat16) for part in parts]
+        scores = [
+            lax.dot_general(f, k, (((1,), (1,)), ((), ())), preferred_element_type=jnp.float32)
+            for f, k in zip(feats, keys)
+        ]
         at = lax.broadcasted_iota(jnp.int32, (T, T), 0)
         of = lax.broadcasted_iota(jnp.int32, (T, T), 1)
-        scores = jnp.where(at >= of, scores, 0.0).astype(jnp.bfloat16)
-        v = vals[h]
-        joined = jnp.concatenate([v, jnp.ones_like(v)], axis=1)
-        intra[h] = jnp.dot(scores, joined, preferred_element_type=jnp.float32)
-
-    def finish(j, o):
-        h = j * G + o
-        pl.when(o != me)(lambda: r_arrival(j, o).wait_recv())
-        state = r_recv[j, o]
-        weights = state[2 * DH :].astype(jnp.float32)
-        weights = jnp.concatenate([weights[:8], weights[8:]], axis=1)
-        weights = jnp.concatenate([weights, weights], axis=0).astype(jnp.bfloat16)
-        sums = jnp.concatenate([state[:DH], state[DH : 2 * DH]], axis=1)
-        joined = jnp.concatenate([sums] + [weights] * (DH // 16), axis=0)
-        both = intra[h] + lax.dot_general(
-            qf[h], joined, (((1,), (1,)), ((), ())), preferred_element_type=jnp.float32
-        )
-        result = (both[:, :DH] / both[:, DH:]).astype(jnp.bfloat16)
-        outb[:, pl.ds(pl.multiple_of(h * DH, DH), DH)] = result
-
-    def out_cols(j):
-        return pl.ds(pl.multiple_of(j * wide, wide), wide)
-
-    def out_remote(j):
-        return pltpu.make_async_remote_copy(
-            outb.at[pl.ds(pl.multiple_of(other * rows, rows), rows), out_cols(j)],
-            out.at[:, pl.ds(pl.multiple_of(core * half + j * wide, wide), wide)],
-            os_sem.at[j], or_sem.at[j], device_id=mate, device_id_type=MESH,
-        )
-
-    def out_local(j):
+        scores = [jnp.where(at >= of, w, 0.0).astype(jnp.bfloat16) for w in scores]
+        sums = [
+            jnp.dot(
+                w, jnp.concatenate([v, jnp.ones_like(v)], axis=1),
+                preferred_element_type=jnp.float32,
+            )
+            for w, v in zip(scores, vs)
+        ]
+        for h, f, w in zip(heads, feats, sums):
+            qf[h] = f
+            intra[h] = w
+
+    def finish(j, places):
+        for o in places:
+            pl.when(o != me)(lambda o=o: r_arrival(j, o).wait_recv())
+        heads = [j * G + o for o in places]
+        joins = []
+        for o in places:
+            state = r_recv[j, o]
+            weights = state[2 * DH :].astype(jnp.float32)
+            weights = jnp.concatenate([weights[:8], weights[8:]], axis=1)
+            weights = jnp.concatenate([weights, weights], axis=0).astype(jnp.bfloat16)
+            sums = jnp.concatenate([state[:DH], state[DH : 2 * DH]], axis=1)
+            joins.append(jnp.concatenate([sums] + [weights] * (DH // 16), axis=0))
+        both = [
+            intra[h] + lax.dot_general(
+                qf[h], joined, (((1,), (1,)), ((), ())), preferred_element_type=jnp.float32
+            )
+            for h, joined in zip(heads, joins)
+        ]
+        results = [(b[:, :DH] / b[:, DH:]).astype(jnp.bfloat16) for b in both]
+        for h, result in zip(heads, results):
+            outb[:, pl.ds(pl.multiple_of(h * DH, DH), DH)] = result
+
+    piece = wide // 2
+
+    def out_remote(i):
+        return pltpu.make_async_remote_copy(
+            outb.at[
+                pl.ds(pl.multiple_of(other * rows, rows), rows),
+                pl.ds(pl.multiple_of(i * piece, piece), piece),
+            ],
+            out.at[:, pl.ds(pl.multiple_of(core * half + i * piece, piece), piece)],
+            os_sem.at[i], or_sem.at[i], device_id=mate, device_id_type=MESH,
+        )
+
+    def out_local(i):
         return pltpu.make_async_copy(
-            outb.at[pl.ds(pl.multiple_of(core * rows, rows), rows), out_cols(j)],
-            out.at[:, pl.ds(pl.multiple_of(core * half + j * wide, wide), wide)],
-            ol_sem.at[j],
+            outb.at[
+                pl.ds(pl.multiple_of(core * rows, rows), rows),
+                pl.ds(pl.multiple_of(i * piece, piece), piece),
+            ],
+            out.at[:, pl.ds(pl.multiple_of(core * half + i * piece, piece), piece)],
+            ol_sem.at[i],
         )
 
     def over(count, body):
@@ -305,26 +328,65 @@
         moved = pltpu.roll(edge, 3 * a, 0) if a else edge
         x_all[a, pl.ds(0, RIM), :] = moved.astype(x_all.dtype)
 
-    def first(j):
-        exchange(1, j).wait_recv()
-        exchange(2, j).wait_recv()
-        over(G, lambda i: keys_and_sums(j, ordered(i)))
-
-    over(J, first)
-
-    def middle(j):
-        own(j)
-        exchange(0, j).wait_recv()
-        over(G, lambda o: within(j, o))
-
-    over(J, middle)
-
-    def last(j):
-        over(G, lambda o: finish(j, o))
-        out_remote(j).start()
-        out_local(j).start()
-
-    over(J, last)
+    pairs = G // 4
+    steps = 4 * J
+    lag = jnp.minimum(z, steps - 2 * J - 2)
+
+    def step(t):
+        j = lax.rem(t // 2, J)
+        low = lax.rem(t, 2) * (G // 2)
+
+        @pl.when(t < 2 * J)
+        def _():
+            @pl.when(lax.rem(t, 2) == 0)
+            def _():
+                exchange(1, j).wait_recv()
+                exchange(2, j).wait_recv()
+
+            def one(p):
+                i = low + 2 * p
+                places = [ordered(i), ordered(i + 1)]
+                keys_and_sums(j, places)
+                s_copy(j, places[0]).start()
+                pl.when(i + 1 < G - 1)(lambda: s_copy(j, places[1]).start())
+
+            over(pairs, one)
+
+            @pl.when(lax.rem(t, 2) == 1)
+            def _():
+                s_recv[j, me] = s_send[j, me]
+
+        @pl.when(t >= 2 * J)
+        def _():
+            pl.when(lax.rem(t, 2) == 0)(lambda: exchange(0, j).wait_recv())
+
+            def one(p):
+                h = j * G + low + 2 * p
+                within([h, h + 1])
+
+            over(pairs, one)
+
+        due = t - 3 - lag
+
+        @pl.when((due >= 0) & (lax.rem(due, 2) == 0) & (due < 2 * J))
+        def _():
+            own(due // 2)
+
+    over(steps, step)
+
+    def last(i):
+        j = i // 2
+        low = lax.rem(i, 2) * (G // 2)
+
+        def one(p):
+            o = low + 2 * p
+            finish(j, [o, o + 1])
+
+        over(pairs, one)
+        out_remote(i).start()
+        out_local(i).start()
+
+    over(2 * J, last)
 
     for k in range(CORES):
         pl.when(has_next)(lambda k=k: rim(k).wait_send())
@@ -341,8 +403,9 @@
 
         over(G, one)
         pl.when(z < Z - 1)(lambda: chain(j).wait_send())
-        out_remote(j).wait()
-        out_local(j).wait()
+        for i in range(2):
+            out_remote(2 * j + i).wait()
+            out_local(2 * j + i).wait()
 
     over(J, drain)
 
@@ -367,11 +430,7 @@
     return pl.pallas_call(
         functools.partial(kernel, plan),
         out_shape=jax.ShapeDtypeStruct((rows, width), bf16),
-        in_specs=[
-            pl.BlockSpec(memory_space=pl.ANY),
-            pl.BlockSpec(memory_space=pl.ANY),
-            pl.BlockSpec(memory_space=pl.ANY),
-        ],
+        in_specs=[pl.BlockSpec(memory_space=pltpu.HBM)] * 3,
         out_specs=pl.BlockSpec(memory_space=pl.ANY),
         scratch_shapes=[
             pltpu.VMEM((3, RIM + T, half), bf16),
@@ -395,15 +454,15 @@
             dma((slots, group)), dma((slots, group)),
             dma((slots,)), dma((slots,)),
             dma((slots, group)), dma((slots, group)),
-            dma((slots,)), dma((slots,)), dma((slots,)),
+            dma((2 * slots,)), dma((2 * slots,)), dma((2 * slots,)),
         ],
         compiler_params=pltpu.CompilerParams(
-            collective_id=0, has_side_effects=True, vmem_limit_bytes=60 * 1024 * 1024
+            collective_id=0, has_side_effects=True, vmem_limit_bytes=40 * 1024 * 1024
         ),
         cost_estimate=pl.CostEstimate(
             flops=2_000_000_000, bytes_accessed=8_000_000, transcendentals=2_000_000
         ),
-    )(projected, conv_filter, frequencies)
+    )(*[pltpu.with_memory_space_constraint(a, pltpu.HBM) for a in (projected, conv_filter, frequencies)])
 
 
 def solution(mesh):

time: 39.5 us -> 42.7 us (1.081)
  Pallas kernels: 37.1 us -> 41.1 us
  local copies, waits for them, and re-layouts: 2.29 us -> 0.97 us
    pallas_call x1, Pallas kernels: 37.1 us -> 41.1 us  [per_device(): pl.pallas_call(functools.partial(kernel, plan), out_shape=jax.ShapeDtypeS...]
    unnamed x1, local copies, waits for them, and re-layouts: 2.29 us -> 0.97 us
where the time goes in v3:
time: 42.7 us; the launch traced here: 42.1 us
  Pallas kernels  41.1 us (96%)
  local copies, waits for them, and re-layouts  0.97 us (2%)
    pallas_call x1, Pallas kernels, per_device(): pl.pallas_call(functools.partial(kernel, plan), out_shape=jax.ShapeDtypeS...  41.1 us
    unnamed x1, local copies, waits for them, and re-layouts  0.97 us

profile of v3, /device:TPU:29, one launch (start us, length us, event | category | flops | bytes accessed | tf_op | source)
XLA Modules:
  0.0 42.1 jit_solution(1790380567486167022)
XLA Ops:
  0.0 41.1 %shard_map.37 = bf16[128,4096]{1,0:T(8,128)(2,1)S(1)} custom-call(bf16[3,128,4096]{2,1,0:T(8,128)(2,1)} %proj.1, f32[3,4,4096]{2,1,0:T(4,128)} %filt.1, bf16[32,128,256]{2,1,0:T(8,128)(2,1)} %freq.1), custom_call_target="tpu_custom_call" | custom-call | flops 2000000000 | bytes 8000000 | tf_op jit(solution)/shard_map/pallas_call | solution.py:430
  41.2 1.0 %copy.5 = bf16[128,4096]{1,0:T(8,128)(2,1)} copy(bf16[128,4096]{1,0:T(8,128)(2,1)S(1)} %shard_map.37) | data formatting | bytes 2097152

commit v4 on v3

--- a/solution.py
+++ b/solution.py
@@ -10,6 +10,7 @@
 DH = 128
 M = 256
 KC = 4
+LOG2E = 1.4426950408889634
 CORES = 2
 RIM = 16
 SROWS = 2 * DH + 16
@@ -177,15 +178,16 @@
         ]
         wides = [k.astype(jnp.float32) for k in ks]
         norms = [
-            jnp.sum(w * w, axis=1, keepdims=True) * (0.5 * scale * scale) for w in wides
+            jnp.sum(w * w, axis=1, keepdims=True) * (0.5 * scale * scale * LOG2E) for w in wides
         ]
         feats = [
-            jnp.exp(part * scale - norm).astype(jnp.bfloat16) for part, norm in zip(parts, norms)
+            jnp.exp2(part * (scale * LOG2E) - norm).astype(jnp.bfloat16)
+            for part, norm in zip(parts, norms)
         ]
         sums = [
-            lax.dot_general(
-                jnp.concatenate([v, jnp.ones_like(v)], axis=1), f,
-                (((0,), (0,)), ((), ())), preferred_element_type=jnp.float32,
+            jnp.dot(
+                jnp.concatenate([v.T, jnp.ones((16, T), v.dtype)], axis=0), f,
+                preferred_element_type=jnp.float32,
             )
             for v, f in zip(vs, feats)
         ]
@@ -244,14 +246,26 @@
         parts = [
             jnp.dot(q, omega[h], preferred_element_type=jnp.float32) for q, h in zip(qs, heads)
         ]
-        feats = [jnp.exp(part * scale).astype(jnp.bfloat16) for part in parts]
+        feats = [jnp.exp2(part * (scale * LOG2E)).astype(jnp.bfloat16) for part in parts]
         scores = [
             lax.dot_general(f, k, (((1,), (1,)), ((), ())), preferred_element_type=jnp.float32)
             for f, k in zip(feats, keys)
         ]
-        at = lax.broadcasted_iota(jnp.int32, (T, T), 0)
-        of = lax.broadcasted_iota(jnp.int32, (T, T), 1)
-        scores = [jnp.where(at >= of, w, 0.0).astype(jnp.bfloat16) for w in scores]
+        at = lax.broadcasted_iota(jnp.int32, (rows, rows), 0)
+        of = lax.broadcasted_iota(jnp.int32, (rows, rows), 1)
+        causal = at >= of
+        never = jnp.zeros((rows, rows), jnp.bfloat16)
+
+        def masked(w):
+            first = jnp.where(causal, w[:rows, :rows], 0.0).astype(jnp.bfloat16)
+            second = jnp.where(causal, w[rows:, rows:], 0.0).astype(jnp.bfloat16)
+            under = w[rows:, :rows].astype(jnp.bfloat16)
+            return jnp.concatenate(
+                [jnp.concatenate([first, never], axis=1), jnp.concatenate([under, second], axis=1)],
+                axis=0,
+            )
+
+        scores = [masked(w) for w in scores]
         sums = [
             jnp.dot(
                 w, jnp.concatenate([v, jnp.ones_like(v)], axis=1),
@@ -330,7 +344,7 @@
 
     pairs = G // 4
     steps = 4 * J
-    lag = jnp.minimum(z, steps - 2 * J - 2)
+    lag = jnp.minimum(2 * z, steps - 2 * J - 2)
 
     def step(t):
         j = lax.rem(t // 2, J)

time: 42.7 us -> 42.7 us (level)
  no operation moved by 1% of the time
where the time goes in v4:
time: 42.7 us; the launch traced here: 42.1 us
  Pallas kernels  41.1 us (96%)
  local copies, waits for them, and re-layouts  0.97 us (2%)
    pallas_call x1, Pallas kernels, per_device(): pl.pallas_call(functools.partial(kernel, plan), out_shape=jax.ShapeDtypeS...  41.1 us
    unnamed x1, local copies, waits for them, and re-layouts  0.97 us

profile of v4, /device:TPU:29, one launch (start us, length us, event | category | flops | bytes accessed | tf_op | source)
XLA Modules:
  0.0 42.1 jit_solution(1620978496647428705)
XLA Ops:
  0.0 41.1 %shard_map.37 = bf16[128,4096]{1,0:T(8,128)(2,1)S(1)} custom-call(bf16[3,128,4096]{2,1,0:T(8,128)(2,1)} %proj.1, f32[3,4,4096]{2,1,0:T(4,128)} %filt.1, bf16[32,128,256]{2,1,0:T(8,128)(2,1)} %freq.1), custom_call_target="tpu_custom_call" | custom-call | flops 2000000000 | bytes 8000000 | tf_op jit(solution)/shard_map/pallas_call | solution.py:444
  41.1 1.0 %copy.5 = bf16[128,4096]{1,0:T(8,128)(2,1)} copy(bf16[128,4096]{1,0:T(8,128)(2,1)S(1)} %shard_map.37) | data formatting | bytes 2097152
